TPU v7x, 32 devices: a whole 2x2x4 slice. The times are simulated.
32 devices in a mesh: fsdp: 4 (over y, x), ctx: 4 (over z), blk: 2 (over core).
Axes of the slice: x: 2, y: 2, z: 4, core: 2. Of those that a mesh axis runs over, the one named last changes fastest.
Arguments:
- latents: bfloat16 [4, 1024, 1152], P('fsdp', ('ctx', 'blk')), may hold values from -6 to 6
- text_embed: bfloat16 [4, 120, 1152], P('fsdp'), may hold values from -6 to 6
- timestep: float32 [4, 6912], P('fsdp'), may hold values from -1.5 to 1.5
- ada_table: bfloat16 [6, 1152], P(None, 'fsdp'), may hold values from -1.5 to 1.5
- w_attn_in: bfloat16 [1152, 3456], P('fsdp'), may hold values from -0.1875 to 0.1875
- w_attn_out: bfloat16 [1152, 1152], P('fsdp'), may hold values from -2 to 2
- w_cross_q: bfloat16 [1152, 1152], P('fsdp'), may hold values from -0.1875 to 0.1875
- w_cross_kv: bfloat16 [1152, 2304], P('fsdp'), may hold values from -0.1875 to 0.1875
- w_cross_out: bfloat16 [1152, 1152], P('fsdp'), may hold values from -0.75 to 0.75
- w_mlp_up: bfloat16 [1152, 4608], P('fsdp'), may hold values from -0.1875 to 0.1875
- w_mlp_down: bfloat16 [4608, 1152], P('fsdp'), may hold values from -0.09375 to 0.09375
- grad_out: bfloat16 [4, 1024, 1152], P('fsdp', ('ctx', 'blk')), may hold values from -6 to 6
Outputs:
- block_out: bfloat16 [4, 1024, 1152], P('fsdp', ('ctx', 'blk'))
- grad_latents: float32 [4, 1024, 1152], P('fsdp', ('ctx', 'blk'))
- grad_text: float32 [4, 120, 1152], P('fsdp')
- grad_timestep: float32 [4, 6912], P('fsdp')
- grad_table: float32 [6, 1152], P(None, ('fsdp', 'ctx', 'blk'))
- grad_attn_in: float32 [1152, 3456], P(('fsdp', 'ctx', 'blk'))
- grad_attn_out: float32 [1152, 1152], P(('fsdp', 'ctx', 'blk'))
- grad_cross_q: float32 [1152, 1152], P(('fsdp', 'ctx', 'blk'))
- grad_cross_kv: float32 [1152, 2304], P(('fsdp', 'ctx', 'blk'))
- grad_cross_out: float32 [1152, 1152], P(('fsdp', 'ctx', 'blk'))
- grad_mlp_up: float32 [1152, 4608], P(('fsdp', 'ctx', 'blk'))
- grad_mlp_down: float32 [4608, 1152], P(('fsdp', 'ctx', 'blk'))
- grad_shift_mlp: float32 [1152], P(('fsdp', 'ctx', 'blk'))
All inputs are finite; a program needn't handle non-finite values.
Results may differ from a plain program's by a relative error of at most 0.023.
Values may be sent and summed in bfloat16 or wider, within the bound.
No kernel may reach another device: no remote copies, remote signals or barrier semaphores. Data moves between devices by JAX's collectives and lax.ppermute only.
A program may use at most 256 MiB of HBM per device.

v0:
```python
import jax
import jax.numpy as jnp
from jax import lax
from jax.sharding import PartitionSpec as P

D = 1152
HEADS = 16
HEAD = 72
TEXT = 120


epsilon = 1e-06
bfloat = jnp.bfloat16
single = jnp.float32


def layer_norm(values):
    centred = values - jnp.mean(values, axis=-1, keepdims=True)
    variance = jnp.mean(centred * centred, axis=-1, keepdims=True)
    inverse = lax.rsqrt(variance + epsilon)
    return (centred * inverse, inverse)


def norm_back(grad_normed, normed, inverse):
    first_mean = jnp.mean(grad_normed, axis=-1, keepdims=True)
    second_mean = jnp.mean(grad_normed * normed, axis=-1, keepdims=True)
    return inverse * (grad_normed - first_mean - normed * second_mean)


def product(left, right, pattern):
    return jnp.einsum(pattern, left, right, preferred_element_type=single)


def attend_forward(queries, keys_all, values_all, row_block, scaling):
    blocks = queries.shape[0] // row_block

    def one_block(query_block):
        scores = scaling * product(query_block, keys_all, "qhe,khe->hqk")
        maxima = jnp.max(scores, axis=-1, keepdims=True)
        exponent = jnp.exp(scores - maxima)
        summed = jnp.sum(exponent, axis=-1, keepdims=True)
        weights = (exponent / summed).astype(bfloat)
        mixed = product(weights, values_all, "hqk,khe->qhe").astype(bfloat)
        return (mixed, (maxima + jnp.log(summed))[..., 0])

    mixed, log_norm = lax.map(
        one_block, queries.reshape(blocks, row_block, queries.shape[1], queries.shape[2])
    )
    return (mixed.reshape(queries.shape), log_norm)


def attend_backward(queries, keys_all, values_all, grad_mixed, log_norm, row_block, scaling):
    blocks = queries.shape[0] // row_block

    def one_block(carried, inputs_one):
        query_block, grad_block, norm_block = inputs_one
        scores = scaling * product(query_block, keys_all, "qhe,khe->hqk")
        weights = jnp.exp(scores - norm_block[..., None])
        grad_weights = product(grad_block, values_all, "qhe,khe->hqk")
        grad_values = product(weights.astype(bfloat), grad_block, "hqk,qhe->khe")
        inner = jnp.sum(weights * grad_weights, axis=-1, keepdims=True)
        grad_scores = (weights * (grad_weights - inner)).astype(bfloat)
        grad_query = (scaling * product(grad_scores, keys_all, "hqk,khe->qhe")).astype(bfloat)
        grad_keys = scaling * product(grad_scores, query_block, "hqk,qhe->khe")
        return ((carried[0] + grad_keys, carried[1] + grad_values), grad_query)

    shape_tail = (queries.shape[1], queries.shape[2])
    initial = (jnp.zeros(keys_all.shape, single), jnp.zeros(keys_all.shape, single))
    sliced = (
        queries.reshape((blocks, row_block) + shape_tail),
        grad_mixed.reshape((blocks, row_block) + shape_tail),
        log_norm,
    )
    (grad_keys, grad_values), grad_query = lax.scan(one_block, initial, sliced)
    return (grad_query.reshape(queries.shape), grad_keys, grad_values)


def shards(
    latents,
    text_embed,
    timestep,
    ada_table,
    w_attn_in,
    w_attn_out,
    w_cross_q,
    w_cross_kv,
    w_cross_out,
    w_mlp_up,
    w_mlp_down,
    grad_out,
):
    ctx_size = lax.axis_size("ctx")
    blk_size = lax.axis_size("blk")
    batch_dev = latents.shape[0]
    tok_dev = latents.shape[1]
    heads_here = HEADS // ctx_size
    group_rows = tok_dev * ctx_size
    row_block = min(512, group_rows)
    scaling = HEAD ** (-0.5)
    gathered = (
        lax.all_gather(ada_table, "fsdp", axis=1, tiled=True),
        lax.all_gather(w_attn_in, "fsdp", axis=0, tiled=True),
        lax.all_gather(w_attn_out, "fsdp", axis=0, tiled=True),
        lax.all_gather(w_cross_q, "fsdp", axis=0, tiled=True),
        lax.all_gather(w_cross_kv, "fsdp", axis=0, tiled=True),
        lax.all_gather(w_cross_out, "fsdp", axis=0, tiled=True),
        lax.all_gather(w_mlp_up, "fsdp", axis=0, tiled=True),
        lax.all_gather(w_mlp_down, "fsdp", axis=0, tiled=True),
    )
    table_full, attn_in, attn_out, cross_q, cross_kv, cross_out, mlp_up, mlp_down = gathered
    latent_f32 = latents.astype(single)
    modulation = table_full.astype(single)[None] + timestep.reshape(batch_dev, 6, D)
    shift_one = modulation[:, 0, None]
    scale_one = modulation[:, 1, None]
    gate_one = modulation[:, 2, None]
    shift_two = modulation[:, 3, None]
    scale_two = modulation[:, 4, None]
    gate_two = modulation[:, 5, None]
    normed_one, inverse_one = layer_norm(latent_f32)
    modulated_one = (normed_one * (1.0 + scale_one) + shift_one).astype(bfloat)
    packed = product(modulated_one, attn_in, "btd,de->bte").astype(bfloat)
    packed = packed.reshape(batch_dev, tok_dev, 3, ctx_size, heads_here * HEAD)
    head_major = lax.all_to_all(packed, "ctx", split_axis=3, concat_axis=1, tiled=True)
    head_major = head_major.reshape(batch_dev, group_rows, 3, heads_here, HEAD)
    query_all = head_major[:, :, 0]
    pair_all = lax.all_gather(head_major[:, :, 1:], "blk", axis=1, tiled=True)
    keys_all = pair_all[:, :, 0]
    values_all = pair_all[:, :, 1]
    latent_index = 0
    mixed_one, norm_one = attend_forward(
        query_all[latent_index],
        keys_all[latent_index],
        values_all[latent_index],
        row_block,
        scaling,
    )
    mixed_list = [mixed_one]
    norm_list = [norm_one]
    mixed_heads = jnp.stack(mixed_list, 0)
    back_tokens = lax.all_to_all(
        mixed_heads.reshape(batch_dev, group_rows, 1, heads_here * HEAD),
        "ctx",
        split_axis=1,
        concat_axis=2,
        tiled=True,
    )
    back_tokens = back_tokens.reshape(batch_dev, tok_dev, D)
    branch_one = product(back_tokens, attn_out, "btd,de->bte")
    first = latent_f32 + gate_one * branch_one
    first_low = first.astype(bfloat)
    cross_query = (
        product(first_low, cross_q, "btd,de->bte")
        .astype(bfloat)
        .reshape(batch_dev, tok_dev, HEADS, HEAD)
    )
    cross_pairs = (
        product(text_embed, cross_kv, "bsd,de->bse")
        .astype(bfloat)
        .reshape(batch_dev, TEXT, 2, HEADS, HEAD)
    )
    cross_scores = scaling * product(cross_query, cross_pairs[:, :, 0], "bqhe,bkhe->bhqk")
    cross_max = jnp.max(cross_scores, axis=-1, keepdims=True)
    cross_exp = jnp.exp(cross_scores - cross_max)
    cross_weights = cross_exp / jnp.sum(cross_exp, axis=-1, keepdims=True)
    cross_low = cross_weights.astype(bfloat)
    cross_mixed = (
        product(cross_low, cross_pairs[:, :, 1], "bhqk,bkhe->bqhe")
        .astype(bfloat)
        .reshape(batch_dev, tok_dev, D)
    )
    second = first + product(cross_mixed, cross_out, "btd,de->bte")
    normed_two, inverse_two = layer_norm(second)
    modulated_two = (normed_two * (1.0 + scale_two) + shift_two).astype(bfloat)
    hidden_pre = product(modulated_two, mlp_up, "btd,df->btf")
    hidden, gelu_back = jax.vjp(lambda values: jax.nn.gelu(values, approximate=True), hidden_pre)
    hidden_low = hidden.astype(bfloat)
    mlp_branch = product(hidden_low, mlp_down, "btf,fd->btd")
    block_out = (second + gate_two * mlp_branch).astype(bfloat)
    cotangent = grad_out.astype(single)
    grad_gate_two = jnp.sum(cotangent * mlp_branch, axis=1)
    grad_branch_two = (gate_two * cotangent).astype(bfloat)
    grad_mlp_down = product(hidden_low, grad_branch_two, "btf,btd->fd")
    grad_hidden = product(grad_branch_two, mlp_down, "btd,fd->btf")
    grad_pre = gelu_back(grad_hidden)[0].astype(bfloat)
    grad_mlp_up = product(modulated_two, grad_pre, "btd,btf->df")
    grad_mod_two = product(grad_pre, mlp_up, "btf,df->btd")
    grad_scale_two = jnp.sum(grad_mod_two * normed_two, axis=1)
    grad_shift_two = jnp.sum(grad_mod_two, axis=1)
    grad_second = cotangent + norm_back(grad_mod_two * (1.0 + scale_two), normed_two, inverse_two)
    grad_cross_branch = grad_second.astype(bfloat)
    grad_cross_out = product(cross_mixed, grad_cross_branch, "btd,bte->de")
    grad_cross_mixed = (
        product(grad_cross_branch, cross_out, "bte,de->btd")
        .astype(bfloat)
        .reshape(batch_dev, tok_dev, HEADS, HEAD)
    )
    grad_cross_weights = product(grad_cross_mixed, cross_pairs[:, :, 1], "bqhe,bkhe->bhqk")
    grad_cross_values = product(cross_low, grad_cross_mixed, "bhqk,bqhe->bkhe")
    inner_cross = jnp.sum(cross_weights * grad_cross_weights, axis=-1, keepdims=True)
    grad_cross_scores = (cross_weights * (grad_cross_weights - inner_cross)).astype(bfloat)
    grad_cross_query = (
        scaling * product(grad_cross_scores, cross_pairs[:, :, 0], "bhqk,bkhe->bqhe")
    ).astype(bfloat)
    grad_cross_query = grad_cross_query.reshape(batch_dev, tok_dev, D)
    grad_cross_keys = scaling * product(grad_cross_scores, cross_query, "bhqk,bqhe->bkhe")
    grad_cross_q = product(first_low, grad_cross_query, "btd,bte->de")
    grad_first = grad_second + product(grad_cross_query, cross_q, "bte,de->btd")
    grad_gate_one = jnp.sum(grad_first * branch_one, axis=1)
    grad_branch_one = (gate_one * grad_first).astype(bfloat)
    grad_attn_out = product(back_tokens, grad_branch_one, "btd,bte->de")
    grad_mixed_tok = product(grad_branch_one, attn_out, "bte,de->btd").astype(bfloat)
    grad_mixed_heads = lax.all_to_all(
        grad_mixed_tok.reshape(batch_dev, tok_dev, ctx_size, heads_here * HEAD),
        "ctx",
        split_axis=2,
        concat_axis=1,
        tiled=True,
    )
    grad_mixed_heads = grad_mixed_heads.reshape(batch_dev, group_rows, heads_here, HEAD)
    latent_index = 0
    grad_query, grad_keys, grad_values = attend_backward(
        query_all[latent_index],
        keys_all[latent_index],
        values_all[latent_index],
        grad_mixed_heads[latent_index],
        norm_list[latent_index],
        row_block,
        scaling,
    )
    query_grads = [grad_query]
    pair_grads = [jnp.stack([grad_keys, grad_values], 1)]
    pair_summed = lax.psum_scatter(
        jnp.stack(pair_grads, 0).astype(jnp.bfloat16), "blk", scatter_dimension=1, tiled=True
    ).astype(jnp.float32)
    grad_packed = jnp.concatenate(
        [jnp.stack(query_grads, 0)[:, :, None], pair_summed.astype(bfloat)], axis=2
    )
    grad_tok = lax.all_to_all(
        grad_packed.reshape(batch_dev, group_rows, 3, 1, heads_here * HEAD),
        "ctx",
        split_axis=1,
        concat_axis=3,
        tiled=True,
    )
    grad_tok = grad_tok.reshape(batch_dev, tok_dev, 3 * D)
    grad_attn_in = product(modulated_one, grad_tok, "btd,bte->de")
    grad_mod_one = product(grad_tok, attn_in, "bte,de->btd")
    grad_scale_one = jnp.sum(grad_mod_one * normed_one, axis=1)
    grad_shift_one = jnp.sum(grad_mod_one, axis=1)
    grad_latents = grad_first + norm_back(grad_mod_one * (1.0 + scale_one), normed_one, inverse_one)
    grad_modulation = jnp.stack(
        [
            grad_shift_one,
            grad_scale_one,
            grad_gate_one,
            grad_shift_two,
            grad_scale_two,
            grad_gate_two,
        ],
        axis=1,
    )
    cross_part = jnp.stack([grad_cross_keys, grad_cross_values], axis=2).reshape(
        batch_dev, TEXT, 2 * D
    )
    cross_total, stamp_total = (
        lax.psum(cross_part.astype(jnp.bfloat16), ("ctx", "blk")).astype(jnp.float32),
        lax.psum(grad_modulation.astype(jnp.bfloat16), ("ctx", "blk")).astype(jnp.float32),
    )
    grad_pairs = cross_total.astype(bfloat)
    grad_text = product(grad_pairs, cross_kv, "bse,de->bsd")
    grad_cross_kv = product(text_embed, grad_pairs, "bsd,bse->de") / (ctx_size * blk_size)
    grad_timestep = stamp_total.reshape(batch_dev, 6 * D)
    grad_table = jnp.sum(grad_modulation, axis=0)
    owned_rows = (
        lax.psum_scatter(grad_table, ("fsdp", "ctx", "blk"), scatter_dimension=1, tiled=True),
        lax.psum_scatter(grad_attn_in, ("fsdp", "ctx", "blk"), scatter_dimension=0, tiled=True),
        lax.psum_scatter(grad_attn_out, ("fsdp", "ctx", "blk"), scatter_dimension=0, tiled=True),
        lax.psum_scatter(grad_cross_q, ("fsdp", "ctx", "blk"), scatter_dimension=0, tiled=True),
        lax.psum_scatter(grad_cross_kv, ("fsdp", "ctx", "blk"), scatter_dimension=0, tiled=True),
        lax.psum_scatter(grad_cross_out, ("fsdp", "ctx", "blk"), scatter_dimension=0, tiled=True),
        lax.psum_scatter(grad_mlp_up, ("fsdp", "ctx", "blk"), scatter_dimension=0, tiled=True),
        lax.psum_scatter(grad_mlp_down, ("fsdp", "ctx", "blk"), scatter_dimension=0, tiled=True),
    )
    return (
        block_out,
        grad_latents,
        grad_text,
        grad_timestep,
        owned_rows[0],
        owned_rows[1],
        owned_rows[2],
        owned_rows[3],
        owned_rows[4],
        owned_rows[5],
        owned_rows[6],
        owned_rows[7],
        owned_rows[0][3],
    )


def solution(mesh):
    placed = (
        P("fsdp", ("ctx", "blk"), None),
        P("fsdp", None, None),
        P("fsdp", None),
        P(None, "fsdp"),
        P("fsdp", None),
        P("fsdp", None),
        P("fsdp", None),
        P("fsdp", None),
        P("fsdp", None),
        P("fsdp", None),
        P("fsdp", None),
        P("fsdp", ("ctx", "blk"), None),
    )
    return jax.shard_map(
        shards,
        mesh=mesh,
        in_specs=placed,
        out_specs=(
            P("fsdp", ("ctx", "blk"), None),
            P("fsdp", ("ctx", "blk"), None),
            P("fsdp", None, None),
            P("fsdp", None),
            P(None, ("fsdp", "ctx", "blk")),
            P(("fsdp", "ctx", "blk"), None),
            P(("fsdp", "ctx", "blk"), None),
            P(("fsdp", "ctx", "blk"), None),
            P(("fsdp", "ctx", "blk"), None),
            P(("fsdp", "ctx", "blk"), None),
            P(("fsdp", "ctx", "blk"), None),
            P(("fsdp", "ctx", "blk"), None),
            P(("fsdp", "ctx", "blk")),
        ),
        check_vma=False,
    )
```

profile of v0, /device:TPU:4, one launch (start us, length us, event | category | flops | bytes accessed | tf_op | source)
XLA Modules:
  0.0 2098.7 jit_solution(15057810835861781466)
XLA Ops:
  18.1 77.1 %all-gather.10.cloned.1.call-done = bf16[1152,3456]{1,0:T(8,128)(2,1)} async-done(((bf16[288,3456]{1,0:T(8,128)(2,1)}), bf16[1152,3456]{1,0:T(8,128)(2,1)}) %all-gather.10.cloned.1.call-update) | async-done | bytes 7962640 | tf_op jit(solution)/shard_map/all_gather | solution.py:102
  101.0 26.6 %all_to_all.60 = bf16[1,128,3,4,288]{1,4,2,0,3:T(8,128)(2,1)S(1)} all-to-all(bf16[1,128,3,4,288]{1,4,2,0,3:T(8,128)(2,1)S(1)} %copy.59), channel_id=1, replica_groups=mesh['fsdp'=4,'ctx'=4,'blk'=2] {'ctx'}, dimensions={3} | all-to-all | bytes 1769472 | tf_op jit(solution)/shard_map/all_to_all | solution.py:123
  156.0 45.8 %all-gather.16.cloned.1.call-done = bf16[1152,2304]{1,0:T(8,128)(2,1)} async-done(((bf16[288,2304]{1,0:T(8,128)(2,1)}), bf16[1152,2304]{1,0:T(8,128)(2,1)}) %all-gather.16.cloned.1.call-update) | async-done | bytes 5308432 | tf_op jit(solution)/shard_map/all_gather | solution.py:105
  208.5 35.0 %all-gather.14.cloned.1.call-done = bf16[1152,1152]{1,0:T(8,128)(2,1)} async-done(((bf16[288,1152]{1,0:T(8,128)(2,1)}), bf16[1152,1152]{1,0:T(8,128)(2,1)}) %all-gather.14.cloned.1.call-update) | async-done | bytes 2654224 | tf_op jit(solution)/shard_map/all_gather | solution.py:103
  246.0 39.2 %all-gather.18.cloned.1.call-done = bf16[1152,1152]{1,0:T(8,128)(2,1)} async-done(((bf16[288,1152]{1,0:T(8,128)(2,1)}), bf16[1152,1152]{1,0:T(8,128)(2,1)}) %all-gather.18.cloned.1.call-update) | async-done | bytes 2654224 | tf_op jit(solution)/shard_map/all_gather | solution.py:104
  290.8 36.0 %all-gather.20.cloned.1.call-done = bf16[1152,1152]{1,0:T(8,128)(2,1)} async-done(((bf16[288,1152]{1,0:T(8,128)(2,1)}), bf16[1152,1152]{1,0:T(8,128)(2,1)}) %all-gather.20.cloned.1.call-update) | async-done | bytes 2654224 | tf_op jit(solution)/shard_map/all_gather | solution.py:106
  330.0 104.8 %all-gather.22.cloned.1.call-done = bf16[1152,4608]{1,0:T(8,128)(2,1)} async-done(((bf16[288,4608]{1,0:T(8,128)(2,1)}), bf16[1152,4608]{1,0:T(8,128)(2,1)}) %all-gather.22.cloned.1.call-update) | async-done | bytes 10616848 | tf_op jit(solution)/shard_map/all_gather | solution.py:107
  440.6 102.2 %all-gather.24.cloned.1.call-done = bf16[4608,1152]{1,0:T(8,128)(2,1)} async-done(((bf16[1152,1152]{1,0:T(8,128)(2,1)}), bf16[4608,1152]{1,0:T(8,128)(2,1)}) %all-gather.24.cloned.1.call-update) | async-done | bytes 10616848 | tf_op jit(solution)/shard_map/all_gather | solution.py:108
  610.5 32.6 %all-reduce.16.cloned.1.call-done = bf16[120,2304]{0,1:T(8,128)(2,1)} async-done(((bf16[120,2304]{0,1:T(8,128)(2,1)}), bf16[120,2304]{0,1:T(8,128)(2,1)}) %all-reduce.16.cloned.1.call-update) | async-done | bytes 552976 | tf_op jit(solution)/shard_map/psum | solution.py:266
  670.7 379.7 %fusion.4 = f32[40,4608]{1,0:T(8,128)S(1)} fusion(f32[1152,4608]{1,0:T(8,128)} %fusion.97), kind=kCustom, calls=%all-reduce-scatter.4 | all-reduce-scatter fusion | flops 5898241 | bytes 21970944
  1076.9 16.5 all-to-all-start.3
  1110.2 54.6 %collective-permute-done.34 = f32[40,4608]{1,0:T(8,128)} collective-permute-done((f32[40,4608]{1,0:T(8,128)S(1)}, f32[40,4608]{1,0:T(8,128)}, u32[]{:S(2)}, u32[]{:S(2)}) %collective-permute-start.34) | collective-permute-done | bytes 737312
  1164.8 17.7 concatenate.31
  1196.3 505.7 %fusion.104 = (f32[48,3456]{1,0:T(8,128)S(1)}, f32[48,1152]{1,0:T(8,128)S(1)}, f32[48,1152]{1,0:T(8,128)S(1)}, f32[48,1152]{1,0:T(8,128)S(1)}) fusion(f32[1152,3456]{1,0:T(8,128)} %fusion.94, f32[1152,1152]{1,0:T(8,128)} %fusion.84, f32[1152,1152]{1,0:T(8,128)} %fusion.108, f32[1152,1152]{1,0:T(8,128)} %fusion.68), kind=kCustom, calls=%all-reduce-scatter.5 | all-reduce-scatter fusion | flops 10616833 | bytes 33177600
  1747.5 10.7 collective-permute-done.11
  1765.7 17.2 collective-permute-start.18
  1815.2 25.6 %collective-permute-start.7 = (f32[36,3456]{1,0:T(8,128)}, f32[36,3456]{1,0:T(8,128)}, u32[]{:S(2)}, u32[]{:S(2)}) collective-permute-start(f32[36,3456]{1,0:T(8,128)} %slice.66), channel_id=1, source_target_pairs={{0,8},{1,9},{2,10},{3,11},{4,12},{5,13},{6,14},{7,15},{8,16},{9,17... | collective-permute-start | bytes 1493000
  1840.8 29.3 %psum.15 = bf16[1,6912]{1,0:T(2,128)(2,1)S(1)} all-reduce(bf16[1,6912]{1,0:T(2,128)(2,1)S(1)} %bitcast.270), channel_id=1, replica_groups=mesh['fsdp'=4,'ctx'=4,'blk'=2] {'ctx','blk'}, use_global_device_ids=true, to_apply=%region_22.23 | all-reduce | flops 6912 | bytes 27648 | tf_op jit(solution)/shard_map/psum | solution.py:267
  1870.8 42.7 %all-reduce = f32[6,1152]{1,0:T(8,128)S(1)} all-reduce(f32[6,1152]{1,0:T(8,128)S(1)} %bitcast.266), channel_id=3, replica_groups=mesh['fsdp'=4,'ctx'=4,'blk'=2] {'fsdp','ctx','blk'}, use_global_device_ids=true, to_apply=%region_23.24.clone | all-reduce | flops 6912 | bytes 55296
  1920.8 14.5 concatenate.28
  1935.3 15.0 concatenate.29
  1957.0 14.1 concatenate.30
  1982.5 61.4 %collective-permute-done.3 = f32[48,3456]{1,0:T(8,128)} collective-permute-done((f32[48,3456]{1,0:T(8,128)S(1)}, f32[48,3456]{1,0:T(8,128)}, u32[]{:S(2)}, u32[]{:S(2)}) %collective-permute-start.3) | collective-permute-done | bytes 663584
  2051.2 35.0 %concatenate.27 = f32[420,3456]{1,0:T(8,128)} concatenate(f32[36,3456]{1,0:T(8,128)} %collective-permute-done.7, f32[48,3456]{1,0:T(8,128)S(1)} %collective-permute-done.6, f32[48,3456]{1,0:T(8,128)S(1)} %collective-permute-done.5, f32[48,3456]{1,0:T(8,128)S(1)} %collective-permute-done.4, f32[48,3456]{1,0:T(8,128)} %collective-permute-done.3, f32[48,3456]{1,0:T(8,128)} %copy-done.37, ...), dimensions={0} | concatenate | bytes 11612160
  (359 shorter events, 343.5 us)
Async XLA Ops:
  7.2 88.0 %all-gather.10.cloned.1.call-start = ((), (), s32[]{:S(2)}) async-start(), calls=%async_computation.6 | async-start | bytes 9953280 | tf_op jit(solution)/shard_map/all_gather | solution.py:102
  7.9 129.2 %all-gather.12.cloned.1.call-start = ((), (), s32[]{:S(2)}) async-start(), calls=%async_computation.7 | async-start | bytes 1769472 | tf_op jit(solution)/shard_map/all_gather | solution.py:126
  129.3 72.5 %all-gather.16.cloned.1.call-start = ((), (), s32[]{:S(2)}) async-start(), calls=%async_computation.9 | async-start | bytes 6635520 | tf_op jit(solution)/shard_map/all_gather | solution.py:105
  130.1 113.4 %all-gather.14.cloned.1.call-start = ((), (), s32[]{:S(2)}) async-start(), calls=%async_computation.8 | async-start | bytes 3317760 | tf_op jit(solution)/shard_map/all_gather | solution.py:103
  130.7 154.5 %all-gather.18.cloned.1.call-start = ((), (), s32[]{:S(2)}) async-start(), calls=%async_computation.10 | async-start | bytes 3317760 | tf_op jit(solution)/shard_map/all_gather | solution.py:104
  131.2 195.6 %all-gather.20.cloned.1.call-start = ((), (), s32[]{:S(2)}) async-start(), calls=%async_computation.11 | async-start | bytes 3317760 | tf_op jit(solution)/shard_map/all_gather | solution.py:106
  131.8 303.0 %all-gather.22.cloned.1.call-start = ((), (), s32[]{:S(2)}) async-start(), calls=%async_computation.12 | async-start | bytes 13271040 | tf_op jit(solution)/shard_map/all_gather | solution.py:107
  132.6 410.3 %all-gather.24.cloned.1.call-start = ((), (), s32[]{:S(2)}) async-start(), calls=%async_computation.13 | async-start | bytes 13271040 | tf_op jit(solution)/shard_map/all_gather | solution.py:108
  585.8 485.6 %reduce-scatter.15.cloned.1.call-start = ((), (), s32[]{:S(2)}) async-start(), calls=%async_computation.14 | async-start | bytes 1769472 | tf_op jit(solution)/shard_map/reduce_scatter | solution.py:232
  610.4 1477.8 %all-reduce.18.cloned.1.call-start = ((), (), s32[]{:S(2)}) async-start(), calls=%async_computation.17 | async-start | bytes 21233664
  649.7 1441.6 %reduce-scatter.17.cloned.1.call-start = ((), (), s32[]{:S(2)}) async-start(), calls=%async_computation.16 | async-start | bytes 21897216 | tf_op jit(solution)/shard_map/reduce_scatter | solution.py:282
  1050.4 114.4 %collective-permute-start.34 = (f32[40,4608]{1,0:T(8,128)S(1)}, f32[40,4608]{1,0:T(8,128)}, u32[]{:S(2)}, u32[]{:S(2)}) collective-permute-start(f32[40,4608]{1,0:T(8,128)S(1)} %fusion.4), channel_id=1, source_target_pairs={{0,3},{1,4},{2,5},{3,6},{4,7},{5,8},{6,9},{7,10},{8,11},{9,12},{10... | collective-permute-start | bytes 2211848
  1052.3 112.4 %collective-permute-start.33 = (f32[40,4608]{1,0:T(8,128)S(1)}, f32[40,4608]{1,0:T(8,128)}, u32[]{:S(2)}, u32[]{:S(2)}) collective-permute-start(f32[40,4608]{1,0:T(8,128)S(1)} %fusion.4), channel_id=1, source_target_pairs={{0,2},{1,3},{2,4},{3,5},{4,6},{5,7},{6,8},{7,9},{8,10},{9,11},{10,... | collective-permute-start | bytes 2211848
  1054.3 110.5 %collective-permute-start.32 = (f32[40,4608]{1,0:T(8,128)S(1)}, f32[40,4608]{1,0:T(8,128)}, u32[]{:S(2)}, u32[]{:S(2)}) collective-permute-start(f32[40,4608]{1,0:T(8,128)S(1)} %fusion.4), channel_id=1, source_target_pairs={{0,1},{1,2},{2,3},{3,4},{4,5},{5,6},{6,7},{7,8},{8,9},{9,10},{10,1... | collective-permute-start | bytes 2211848
  1076.9 107.7 %all-to-all-start.3 = ((bf16[1,512,3,1,288]{4,2,3,0,1:T(4,128)(2,1)}), bf16[1,512,3,1,288]{4,2,3,0,1:T(4,128)(2,1)S(1)}, u32[]{:S(2)}, u32[]{:S(2)}) async-start(bf16[1,512,3,1,288]{4,2,3,0,1:T(4,128)(2,1)} %pad_maximum_fusion), calls=%async_computation.4 | async-start | bytes 3145728 | tf_op jit(solution)/shard_map/all_to_all | solution.py:238
  1801.7 171.7 %collective-permute-start.6 = (f32[48,3456]{1,0:T(8,128)S(1)}, f32[48,3456]{1,0:T(8,128)S(1)}, u32[]{:S(2)}, u32[]{:S(2)}) collective-permute-start(f32[48,3456]{1,0:T(8,128)S(1)} %get-tuple-element.128), channel_id=1, source_target_pairs={{0,7},{1,8},{2,9},{3,10},{4,11},{5,12},{6,13},{7,14},{8,15},{9,16}... | collective-permute-start | bytes 1990664
  1803.7 172.0 %collective-permute-start.5 = (f32[48,3456]{1,0:T(8,128)S(1)}, f32[48,3456]{1,0:T(8,128)S(1)}, u32[]{:S(2)}, u32[]{:S(2)}) collective-permute-start(f32[48,3456]{1,0:T(8,128)S(1)} %get-tuple-element.128), channel_id=1, source_target_pairs={{0,6},{1,7},{2,8},{3,9},{4,10},{5,11},{6,12},{7,13},{8,14},{9,15},... | collective-permute-start | bytes 1990664
  1811.3 102.3 %collective-permute-start.27 = (f32[48,1152]{1,0:T(8,128)S(1)}, f32[48,1152]{1,0:T(8,128)}, u32[]{:S(2)}, u32[]{:S(2)}) collective-permute-start(f32[48,1152]{1,0:T(8,128)S(1)} %get-tuple-element.131), channel_id=1, source_target_pairs={{0,4},{1,5},{2,6},{3,7},{4,8},{5,9},{6,10},{7,11},{8,12},{9,13},{1... | collective-permute-start | bytes 663560
  1813.2 105.1 %collective-permute-start.26 = (f32[48,1152]{1,0:T(8,128)S(1)}, f32[48,1152]{1,0:T(8,128)}, u32[]{:S(2)}, u32[]{:S(2)}) collective-permute-start(f32[48,1152]{1,0:T(8,128)S(1)} %get-tuple-element.131), channel_id=1, source_target_pairs={{0,3},{1,4},{2,5},{3,6},{4,7},{5,8},{6,9},{7,10},{8,11},{9,12},{10... | collective-permute-start | bytes 663560
  1815.2 155.9 %collective-permute-start.7 = (f32[36,3456]{1,0:T(8,128)}, f32[36,3456]{1,0:T(8,128)}, u32[]{:S(2)}, u32[]{:S(2)}) collective-permute-start(f32[36,3456]{1,0:T(8,128)} %slice.66), channel_id=1, source_target_pairs={{0,8},{1,9},{2,10},{3,11},{4,12},{5,13},{6,14},{7,15},{8,16},{9,17... | collective-permute-start | bytes 1493000
  1952.9 90.9 %collective-permute-start.3 = (f32[48,3456]{1,0:T(8,128)S(1)}, f32[48,3456]{1,0:T(8,128)}, u32[]{:S(2)}, u32[]{:S(2)}) collective-permute-start(f32[48,3456]{1,0:T(8,128)S(1)} %get-tuple-element.128), channel_id=1, source_target_pairs={{0,4},{1,5},{2,6},{3,7},{4,8},{5,9},{6,10},{7,11},{8,12},{9,13},{1... | collective-permute-start | bytes 1990664
  1971.1 78.4 %collective-permute-start.2 = (f32[48,3456]{1,0:T(8,128)S(1)}, f32[48,3456]{1,0:T(8,128)S(1)}, u32[]{:S(2)}, u32[]{:S(2)}) collective-permute-start(f32[48,3456]{1,0:T(8,128)S(1)} %get-tuple-element.128), channel_id=1, source_target_pairs={{0,3},{1,4},{2,5},{3,6},{4,7},{5,8},{6,9},{7,10},{8,11},{9,12},{10... | collective-permute-start | bytes 1990664
  1973.4 76.1 %collective-permute-start.1 = (f32[48,3456]{1,0:T(8,128)S(1)}, f32[48,3456]{1,0:T(8,128)S(1)}, u32[]{:S(2)}, u32[]{:S(2)}) collective-permute-start(f32[48,3456]{1,0:T(8,128)S(1)} %get-tuple-element.128), channel_id=1, source_target_pairs={{0,2},{1,3},{2,4},{3,5},{4,6},{5,7},{6,8},{7,9},{8,10},{9,11},{10,... | collective-permute-start | bytes 1990664
  1975.7 75.6 %collective-permute-start = (f32[48,3456]{1,0:T(8,128)S(1)}, f32[48,3456]{1,0:T(8,128)}, u32[]{:S(2)}, u32[]{:S(2)}) collective-permute-start(f32[48,3456]{1,0:T(8,128)S(1)} %get-tuple-element.128), channel_id=1, source_target_pairs={{0,1},{1,2},{2,3},{3,4},{4,5},{5,6},{6,7},{7,8},{8,9},{9,10},{10,1... | collective-permute-start | bytes 1990664
  (102 other events, 4510.5 us)
Sparse Core Ops, SparseCore 0:
  9.9 85.2 all-gather.9
  129.5 7.6 all-gather.11
  139.0 62.8 all-gather.15
  203.6 39.9 all-gather.13
  245.2 39.9 all-gather.17
  286.9 39.9 all-gather.19
  328.6 106.1 all-gather.21
  436.7 106.1 all-gather.23
  586.0 57.1 all-reduce.15
  645.2 7.9 reduce-scatter.14
  660.4 320.6 all-reduce.17
  987.9 340.4 reduce-scatter.16
where the time goes:
time: 2110 us; the launch traced here: 2100 us
  blocking collectives  992 us (47%)
  waiting for transfers between devices  634 us (30%)
  starting transfers between devices  167 us (8%)
  local copies, waits for them, and re-layouts  144 us (7%)
  matrix products  127 us (6%)
    unnamed x3, blocking collectives  928 us
    unnamed x49, waiting for transfers between devices  153 us
    unnamed x37, starting transfers between devices  141 us
    dot_general x32, matrix products, product(): return jnp.einsum(pattern, left, right, preferred_element_type=single)  125 us
    unnamed x172, local copies, waits for them, and re-layouts  123 us
    all_gather x1, waiting for transfers between devices, shards(): lax.all_gather(w_mlp_up, 'fsdp', axis=0, tiled=True)  105 us
    all_gather x1, waiting for transfers between devices, shards(): lax.all_gather(w_mlp_down, 'fsdp', axis=0, tiled=True)  102 us
    all_gather x1, waiting for transfers between devices, shards(): lax.all_gather(w_attn_in, 'fsdp', axis=0, tiled=True)  77.1 us
  transfers between devices with their start and end apart: 51, of which 18 were waited for; matrix products, arithmetic and copies ran while one was open for 54% of the time, Pallas kernels for 0%

commit v1 on v0

v1 whole, which is shorter than its diff:
```python
import jax
import jax.numpy as jnp
from jax import lax
from jax.sharding import PartitionSpec as P

D = 1152
HEADS = 16
HEAD = 72
TEXT = 120

epsilon = 1e-06
bfloat = jnp.bfloat16
single = jnp.float32


def layer_norm(values):
    centred = values - jnp.mean(values, axis=-1, keepdims=True)
    variance = jnp.mean(centred * centred, axis=-1, keepdims=True)
    inverse = lax.rsqrt(variance + epsilon)
    return (centred * inverse, inverse)


def norm_back(grad_normed, normed, inverse):
    first_mean = jnp.mean(grad_normed, axis=-1, keepdims=True)
    second_mean = jnp.mean(grad_normed * normed, axis=-1, keepdims=True)
    return inverse * (grad_normed - first_mean - normed * second_mean)


def product(left, right, pattern):
    return jnp.einsum(pattern, left, right, preferred_element_type=single)


def swap(values, axis, step):
    size = lax.axis_size(axis)
    return lax.ppermute(values, axis, [(i, i ^ step) for i in range(size)])


def tree_sum(parts):
    while len(parts) > 1:
        parts = [parts[i] + parts[i + 1] for i in range(0, len(parts), 2)]
    return parts[0]


def pick(values, index):
    return lax.dynamic_index_in_dim(values, index, 0, keepdims=False)


def reorder(parts, index):
    count = len(parts)
    bit = 1
    parts = list(parts)
    while bit < count:
        flag = (index & bit) != 0
        parts = [jnp.where(flag, parts[i ^ bit], parts[i]) for i in range(count)]
        bit *= 2
    return parts


def gather_relative(values, axis):
    size = lax.axis_size(axis)
    return [values] + [swap(values, axis, step) for step in range(1, size)]


def scatter_sum(chunks, axis, own):
    size = lax.axis_size(axis)
    parts = [own] + [swap(chunks(step), axis, step).astype(single) for step in range(1, size)]
    return tree_sum(parts)


def exchange_zb(values):
    z = lax.axis_index("ctx")
    b = lax.axis_index("blk")
    size = values.shape[0]
    by_core = jnp.moveaxis(values, 1, 0)
    keep = pick(by_core, b)
    taken = swap(pick(by_core, 1 - b), "blk", 1)
    pair = jnp.stack([keep, taken], axis=1)
    parts = [pick(pair, z)] + [swap(pick(pair, z ^ step), "ctx", step) for step in range(1, size)]
    nat = jnp.stack(reorder(parts, z), 0)
    return jnp.stack(reorder([nat[:, 0], nat[:, 1]], b), 1)


def rows_permuted(values, f_size, z_size):
    piece = D // (f_size * z_size * 2)
    return (
        values.T.reshape(f_size * z_size, 2, piece, -1).transpose(1, 0, 2, 3).reshape(2, D // 2, -1)
    )


def core_sum(left_t, right):
    b = lax.axis_index("blk")
    send = product(pick(left_t, 1 - b), right, "kt,tn->kn").astype(bfloat)
    keep = product(pick(left_t, b), right, "kt,tn->kn")
    return keep + swap(send, "blk", 1).astype(single)


def plane_sum(half):
    f = lax.axis_index("fsdp")
    f_size = lax.axis_size("fsdp")
    rows = half.reshape(f_size, half.shape[0] // f_size, half.shape[1])
    low = rows.astype(bfloat)
    return scatter_sum(lambda step: pick(low, f ^ step), "fsdp", pick(rows, f))


def depth_sum(rows):
    z = lax.axis_index("ctx")
    low = rows.astype(bfloat)
    return scatter_sum(lambda step: pick(low, z ^ step), "ctx", pick(rows, z))


def shards(
    latents,
    text_embed,
    timestep,
    ada_table,
    w_attn_in,
    w_attn_out,
    w_cross_q,
    w_cross_kv,
    w_cross_out,
    w_mlp_up,
    w_mlp_down,
    grad_out,
):
    f_size = lax.axis_size("fsdp")
    z_size = lax.axis_size("ctx")
    group = 2 * z_size
    f = lax.axis_index("fsdp")
    z = lax.axis_index("ctx")
    b = lax.axis_index("blk")
    g = 2 * z + b
    tok = latents.shape[1]
    total = tok * group
    heads_here = HEADS // group
    wide = heads_here * HEAD
    kv_wide = 2 * D // group
    rows_f = D // f_size
    scaling = HEAD ** (-0.5)

    x = latents[0].astype(single)
    cotangent = grad_out[0].astype(single)
    text = text_embed[0]

    table = jnp.concatenate(reorder(gather_relative(ada_table, "fsdp"), f), axis=1)
    modulation = table.astype(single) + timestep.reshape(6, D)
    shift_one, scale_one, gate_one, shift_two, scale_two, gate_two = [
        modulation[i][None] for i in range(6)
    ]
    normed_one, inverse_one = layer_norm(x)
    modulated_one = (normed_one * (1.0 + scale_one) + shift_one).astype(bfloat)

    own_in = jnp.concatenate(
        [
            lax.dynamic_slice(w_attn_in, (0, i * D + g * wide), (rows_f, wide)) for i in range(3)
        ]
        + [lax.dynamic_slice(w_cross_kv, (0, g * kv_wide), (rows_f, kv_wide))],
        axis=1,
    )
    proj = jnp.concatenate(reorder(gather_relative(own_in, "fsdp"), f), axis=0)
    w_in = proj[:, : 3 * wide]
    w_kv = proj[:, 3 * wide :]

    near = jnp.stack(gather_relative(modulated_one, "ctx"), 0)
    x_all = jnp.stack([near, swap(near, "blk", 1)], 0).reshape(total, D)

    squares = jnp.stack([w_attn_out, w_cross_q, w_cross_out], 0).reshape(3, 2, rows_f // 2, D)
    half = lax.dynamic_index_in_dim(squares, b, 1, keepdims=False)
    square_full = jnp.zeros((3, f_size, 2, rows_f // 2, D), bfloat)
    square_full = lax.dynamic_update_slice(square_full, squares[:, None], (0, f, 0, 0, 0))
    for step in range(1, f_size):
        got = swap(half, "fsdp", step)
        other = swap(got, "blk", 1)
        square_full = lax.dynamic_update_slice(
            square_full, got[:, None, None], (0, f ^ step, b, 0, 0)
        )
        square_full = lax.dynamic_update_slice(
            square_full, other[:, None, None], (0, f ^ step, 1 - b, 0, 0)
        )
    attn_out, cross_q, cross_out = [square_full[i].reshape(D, D) for i in range(3)]

    ff = w_mlp_up.shape[1] // f_size
    up_half = lax.dynamic_slice(w_mlp_up, (b * (rows_f // 2), 0), (rows_f // 2, f_size * ff))
    up_full = jnp.zeros((f_size, 2, rows_f // 2, ff), bfloat)
    up_own = lax.dynamic_slice(w_mlp_up, (0, f * ff), (rows_f, ff)).reshape(1, 2, rows_f // 2, ff)
    up_full = lax.dynamic_update_slice(up_full, up_own, (f, 0, 0, 0))
    for step in range(1, f_size):
        got = swap(
            lax.dynamic_slice(up_half, (0, (f ^ step) * ff), (rows_f // 2, ff)), "fsdp", step
        )
        other = swap(got, "blk", 1)
        up_full = lax.dynamic_update_slice(up_full, got[None, None], (f ^ step, b, 0, 0))
        up_full = lax.dynamic_update_slice(up_full, other[None, None], (f ^ step, 1 - b, 0, 0))
    mlp_up = up_full.reshape(D, ff)
    mlp_down = w_mlp_down

    branch_two_grad = (gate_two * cotangent).astype(bfloat)
    branch_two_all = jnp.concatenate(gather_relative(branch_two_grad, "fsdp"), axis=0)

    pairs_here = product(w_kv, text, "dn,sd->ns").astype(bfloat)
    pairs_near = jnp.stack(reorder(gather_relative(pairs_here, "ctx"), z), 0)
    pairs_all = jnp.stack(reorder([pairs_near, swap(pairs_near, "blk", 1)], b), 1)
    pairs_all = pairs_all.reshape(2, HEADS, HEAD, TEXT)
    text_keys, text_values = pairs_all[0], pairs_all[1]

    packed = product(x_all, w_in, "td,de->te").astype(bfloat)
    packed = packed.reshape(total, 3, heads_here, HEAD)
    query, key, value = packed[:, 0], packed[:, 1], packed[:, 2]
    scores = scaling * product(query, key, "qhe,khe->hqk")
    top = jnp.max(scores, axis=-1, keepdims=True)
    exponent = jnp.exp(scores - top)
    weights = exponent / jnp.sum(exponent, axis=-1, keepdims=True)
    weights_low = weights.astype(bfloat)
    mixed_here = product(weights_low, value, "hqk,khe->heq").astype(bfloat)

    def tokens_to_owner(values):
        n = values.shape[0]
        parts = values.reshape(n, 2, z_size, tok).transpose(1, 2, 0, 3)
        taken = swap(parts[1], "blk", 1)
        pair = jnp.stack([parts[0], taken], axis=1)
        got = [pair[0]] + [swap(pair[step], "ctx", step) for step in range(1, z_size)]
        nat = jnp.stack(reorder(got, z), 0)
        return jnp.stack(reorder([nat[:, 0], nat[:, 1]], b), 1).reshape(group * n, tok)

    def tokens_to_heads(values):
        n = values.shape[0] // group
        parts = values.reshape(z_size, 2, n, tok)
        nat = jnp.stack(reorder([parts[i] for i in range(z_size)], z), 0)
        near = [nat[0]] + [swap(nat[step], "ctx", step) for step in range(1, z_size)]
        near = jnp.stack(near, 0)
        keep, send = reorder([near[:, 0], near[:, 1]], b)
        both = jnp.stack([keep, swap(send, "blk", 1)], 0)
        return both.transpose(2, 0, 1, 3).reshape(n, total)

    mixed_t = tokens_to_owner(mixed_here.reshape(wide, total))
    branch_one = product(mixed_t, attn_out, "dt,de->te")
    first = x + gate_one * branch_one
    first_low = first.astype(bfloat)
    cross_query = product(first_low, cross_q, "td,de->te").astype(bfloat).reshape(tok, HEADS, HEAD)
    cross_scores = scaling * product(cross_query, text_keys, "qhe,hek->hqk")
    cross_max = jnp.max(cross_scores, axis=-1, keepdims=True)
    cross_exp = jnp.exp(cross_scores - cross_max)
    cross_weights = cross_exp / jnp.sum(cross_exp, axis=-1, keepdims=True)
    cross_low = cross_weights.astype(bfloat)
    cross_mixed = product(cross_low, text_values, "hqk,hek->qhe").astype(bfloat).reshape(tok, D)
    second = first + product(cross_mixed, cross_out, "td,de->te")
    normed_two, inverse_two = layer_norm(second)
    modulated_two = (normed_two * (1.0 + scale_two) + shift_two).astype(bfloat)

    x_two_all = jnp.concatenate(gather_relative(modulated_two, "fsdp"), axis=0)
    hidden_pre = product(x_two_all, mlp_up, "td,df->tf")
    hidden, gelu_back = jax.vjp(lambda values: jax.nn.gelu(values, approximate=True), hidden_pre)
    hidden_low = hidden.astype(bfloat)
    grad_hidden = product(branch_two_all, mlp_down, "td,fd->tf")
    grad_pre = gelu_back(grad_hidden)[0].astype(bfloat)

    def from_plane(partial):
        parts = partial.reshape(f_size, tok, D)
        low = parts.astype(bfloat)
        return scatter_sum(lambda step: low[step], "fsdp", parts[0])

    grad_mod_two = from_plane(product(grad_pre, mlp_up, "tf,df->td"))
    mlp_branch = from_plane(product(hidden_low, mlp_down, "tf,fd->td"))
    block_out = (second + gate_two * mlp_branch).astype(bfloat)
    grad_gate_two = jnp.sum(cotangent * mlp_branch, axis=0)

    grad_scale_two = jnp.sum(grad_mod_two * normed_two, axis=0)
    grad_shift_two = jnp.sum(grad_mod_two, axis=0)
    grad_second = cotangent + norm_back(grad_mod_two * (1.0 + scale_two), normed_two, inverse_two)
    grad_cross_branch = grad_second.astype(bfloat)
    grad_cross_mixed = (
        product(grad_cross_branch, cross_out, "te,de->td").astype(bfloat).reshape(tok, HEADS, HEAD)
    )
    grad_cross_weights = product(grad_cross_mixed, text_values, "qhe,hek->hqk")
    grad_cross_values = product(grad_cross_mixed, cross_low, "qhe,hqk->hek")
    inner_cross = jnp.sum(cross_weights * grad_cross_weights, axis=-1, keepdims=True)
    grad_cross_scores = (cross_weights * (grad_cross_weights - inner_cross)).astype(bfloat)
    grad_cross_query = (
        (scaling * product(grad_cross_scores, text_keys, "hqk,hek->qhe"))
        .astype(bfloat)
        .reshape(tok, D)
    )
    grad_cross_keys = scaling * product(cross_query, grad_cross_scores, "qhe,hqk->hek")
    grad_first = grad_second + product(grad_cross_query, cross_q, "te,de->td")
    grad_gate_one = jnp.sum(grad_first * branch_one, axis=0)
    grad_branch_one = (gate_one * grad_first).astype(bfloat)
    grad_mixed_t = product(attn_out, grad_branch_one, "de,te->dt").astype(bfloat)

    grad_mixed = tokens_to_heads(grad_mixed_t).reshape(heads_here, HEAD, total)
    grad_weights = product(grad_mixed, value, "heq,khe->hqk")
    grad_values = product(weights_low, grad_mixed, "hqk,heq->khe")
    inner = jnp.sum(weights * grad_weights, axis=-1, keepdims=True)
    grad_scores = (weights * (grad_weights - inner)).astype(bfloat)
    grad_query = scaling * product(grad_scores, key, "hqk,khe->qhe")
    grad_keys = scaling * product(grad_scores, query, "hqk,qhe->khe")
    grad_packed = (
        jnp.stack([grad_query, grad_keys, grad_values], 1).astype(bfloat).reshape(total, 3 * wide)
    )

    grad_part = product(grad_packed, w_in, "te,de->td").reshape(2, z_size, tok, D)
    grad_near = grad_part[0] + swap(grad_part[1].astype(bfloat), "blk", 1).astype(single)
    grad_near_low = grad_near.astype(bfloat)
    grad_mod_one = scatter_sum(lambda step: grad_near_low[step], "ctx", grad_near[0])
    grad_scale_one = jnp.sum(grad_mod_one * normed_one, axis=0)
    grad_shift_one = jnp.sum(grad_mod_one, axis=0)
    grad_latents = grad_first + norm_back(grad_mod_one * (1.0 + scale_one), normed_one, inverse_one)

    stamp = jnp.stack(
        [
            grad_shift_one,
            grad_scale_one,
            grad_gate_one,
            grad_shift_two,
            grad_scale_two,
            grad_gate_two,
        ],
        axis=0,
    )
    stamp = stamp + swap(stamp, "blk", 1)
    stamp = tree_sum(gather_relative(stamp, "ctx"))
    grad_timestep = stamp.reshape(1, 6 * D)
    table_sum = tree_sum(gather_relative(stamp, "fsdp"))
    own = D // (f_size * group)
    grad_table = lax.dynamic_slice(table_sum, (0, (f * group + g) * own), (6, own))

    pair_grads = jnp.concatenate([grad_cross_keys, grad_cross_values], 0)
    pair_grads = pair_grads.reshape(z_size, 2, kv_wide, TEXT).transpose(1, 0, 2, 3)
    pair_near = pick(pair_grads, b) + swap(pick(pair_grads, 1 - b).astype(bfloat), "blk", 1).astype(single)
    grad_pairs = depth_sum(pair_near).astype(bfloat)
    grad_text_part = product(w_kv, grad_pairs, "dn,ns->ds").reshape(2, D // 2, TEXT)
    text_near = pick(grad_text_part, b) + swap(
        pick(grad_text_part, 1 - b).astype(bfloat), "blk", 1
    ).astype(single)
    text_rows = depth_sum(text_near.reshape(z_size, D // group, TEXT))
    text_rows = jnp.concatenate(reorder(gather_relative(text_rows, "ctx"), z), 0)
    text_rows = jnp.concatenate(reorder([text_rows, swap(text_rows, "blk", 1)], b), 0)
    grad_text = text_rows.T[None]

    def column_parallel(partial):
        rows = partial.reshape(f_size, rows_f, -1)
        low = rows.astype(bfloat)
        mine = scatter_sum(lambda step: pick(low, f ^ step), "fsdp", pick(rows, f)).astype(bfloat)
        got = exchange_zb(mine.reshape(z_size, 2, own, -1)).astype(single)
        return got.reshape(group, own, -1).transpose(1, 0, 2)

    grad_attn_in = column_parallel(product(x_all, grad_packed, "td,te->de"))
    grad_attn_in = (
        grad_attn_in.reshape(own, group, 3, wide).transpose(0, 2, 1, 3).reshape(own, 3 * D)
    )
    grad_cross_kv = column_parallel(product(text, grad_pairs, "sd,ns->dn")).reshape(own, 2 * D)

    def square(left_t, right):
        rows = plane_sum(core_sum(left_t, right))
        return depth_sum(rows.reshape(z_size, own, D))

    grad_attn_out = square(rows_permuted(mixed_t.T, f_size, z_size), grad_branch_one)
    grad_cross_q = square(rows_permuted(first_low, f_size, z_size), grad_cross_query)
    grad_cross_out = square(rows_permuted(cross_mixed, f_size, z_size), grad_cross_branch)

    up_rows = core_sum(rows_permuted(x_two_all, f_size, z_size), grad_pre)
    up_rows = up_rows.astype(bfloat).reshape(f_size, z_size * own, ff)
    up_got = [pick(up_rows, f)] + [
        swap(pick(up_rows, f ^ step), "fsdp", step) for step in range(1, f_size)
    ]
    up_got = jnp.stack(up_got, 0).reshape(f_size, z_size, own, ff).transpose(1, 0, 2, 3)
    up_sum = depth_sum(up_got.astype(single).reshape(z_size, f_size * own, ff))
    up_sum = up_sum.reshape(f_size, own, ff)
    grad_mlp_up = jnp.concatenate(reorder([up_sum[i] for i in range(f_size)], f), axis=1)

    own_down = w_mlp_down.shape[0] // group
    down_t = hidden_low.T.reshape(z_size, 2, own_down, -1).transpose(1, 0, 2, 3)
    down_t = down_t.reshape(2, z_size * own_down, -1)
    down_rows = core_sum(down_t, branch_two_all)
    grad_mlp_down = depth_sum(down_rows.reshape(z_size, own_down, D))

    return (
        block_out[None],
        grad_latents[None],
        grad_text,
        grad_timestep,
        grad_table,
        grad_attn_in,
        grad_attn_out,
        grad_cross_q,
        grad_cross_kv,
        grad_cross_out,
        grad_mlp_up,
        grad_mlp_down,
        grad_table[3],
    )


def solution(mesh):
    placed = (
        P("fsdp", ("ctx", "blk"), None),
        P("fsdp", None, None),
        P("fsdp", None),
        P(None, "fsdp"),
        P("fsdp", None),
        P("fsdp", None),
        P("fsdp", None),
        P("fsdp", None),
        P("fsdp", None),
        P("fsdp", None),
        P("fsdp", None),
        P("fsdp", ("ctx", "blk"), None),
    )
    owned = P(("fsdp", "ctx", "blk"), None)
    return jax.shard_map(
        shards,
        mesh=mesh,
        in_specs=placed,
        out_specs=(
            P("fsdp", ("ctx", "blk"), None),
            P("fsdp", ("ctx", "blk"), None),
            P("fsdp", None, None),
            P("fsdp", None),
            P(None, ("fsdp", "ctx", "blk")),
            owned,
            owned,
            owned,
            owned,
            owned,
            owned,
            owned,
            P(("fsdp", "ctx", "blk")),
        ),
        check_vma=False,
    )
```

time: 2110 us -> 595 us (0.28)
  the two profiles are of different devices: /device:TPU:4 before, /device:TPU:0 now
where the time goes in v1:
time: 595 us; the launch traced here: 584 us
  starting transfers between devices  153 us (26%)
  waiting for transfers between devices  140 us (24%)
  local copies, waits for them, and re-layouts  129 us (22%)
  matrix products  91.3 us (15%)
  other arithmetic  68.3 us (11%)
    ppermute x115, starting transfers between devices, swap(): return lax.ppermute(values, axis, [(i, i ^ step) for i in range(size)])  153 us
    ppermute x115, waiting for transfers between devices, swap(): return lax.ppermute(values, axis, [(i, i ^ step) for i in range(size)])  140 us
    dot_general x36, matrix products, product(): return jnp.einsum(pattern, left, right, preferred_element_type=single)  81.6 us
    unnamed x199, local copies, waits for them, and re-layouts  15 us
    add x10, other arithmetic, tree_sum(): parts = [parts[i] + parts[i + 1] for i in range(0, len(parts), 2)]  13.7 us
    dynamic_slice x13, local copies, waits for them, and re-layouts, pick(): return lax.dynamic_index_in_dim(values, index, 0, keepdims=False)  12.9 us
  transfers between devices with their start and end apart: 115, of which 35 were waited for; matrix products, arithmetic and copies ran while one was open for 46% of the time, Pallas kernels for 0%

profile of v1, /device:TPU:0, one launch (start us, length us, event | category | flops | bytes accessed | tf_op | source)
XLA Modules:
  0.0 584.0 jit_solution(3242370650233477186)
XLA Ops:
  5.0 3.9 collective-permute-start.7
  38.2 9.9 %collective-permute-done.3 = bf16[128,1152]{1,0:T(8,128)(2,1)S(1)} collective-permute-done((bf16[128,1152]{1,0:T(8,128)(2,1)S(1)}, bf16[128,1152]{1,0:T(8,128)(2,1)S(1)}, u32[]{:S(2)}, u32[]{:S(2)}) %collective-permute-start.3) | collective-permute-done | bytes 294944 | tf_op jit(solution)/shard_map/ppermute | solution.py:35
  54.0 4.2 collective-permute-done.5
  66.3 4.6 collective-permute-start.21
  70.9 11.6 %collective-permute-done.27 = bf16[144,1152]{1,0:T(8,128)(2,1)S(1)} collective-permute-done((bf16[144,1152]{1,0:T(8,128)(2,1)S(1)}, bf16[144,1152]{1,0:T(8,128)(2,1)S(1)}, u32[]{:S(2)}, u32[]{:S(2)}) %collective-permute-start.27) | collective-permute-done | bytes 331808 | tf_op jit(solution)/shard_map/ppermute | solution.py:35
  87.8 25.8 %collective-permute-done.29 = bf16[144,1152]{1,0:T(8,128)(2,1)S(1)} collective-permute-done((bf16[144,1152]{1,0:T(8,128)(2,1)S(1)}, bf16[144,1152]{1,0:T(8,128)(2,1)S(1)}, u32[]{:S(2)}, u32[]{:S(2)}) %collective-permute-start.29) | collective-permute-done | bytes 331808 | tf_op jit(solution)/shard_map/ppermute | solution.py:35
  116.5 7.7 %collective-permute-done.31 = bf16[144,1152]{1,0:T(8,128)(2,1)S(1)} collective-permute-done((bf16[144,1152]{1,0:T(8,128)(2,1)S(1)}, bf16[144,1152]{1,0:T(8,128)(2,1)S(1)}, u32[]{:S(2)}, u32[]{:S(2)}) %collective-permute-start.31) | collective-permute-done | bytes 331808 | tf_op jit(solution)/shard_map/ppermute | solution.py:35
  131.0 7.2 %fusion.194 = (f32[2,1024]{1,0:T(2,128)S(1)}, f32[2,1024,1024]{1,2,0:T(8,128)}) fusion(bf16[1024,3,2,72]{0,3,2,1:T(8,128)(2,1)} %bitcast.660), kind=kOutput, calls=%fused_computation.495 | convolution fusion | flops 308282368 | bytes 8986624 | tf_op jit(solution)/shard_map/sub | solution.py:210
  138.8 5.4 fusion.33
  155.4 4.3 copy.479
  178.2 4.6 fusion.190
  215.9 5.1 fusion.20
  244.2 3.9 fusion.12
  256.3 6.3 %collective-permute-done.39 = bf16[128,1152]{1,0:T(8,128)(2,1)S(1)} collective-permute-done((bf16[128,1152]{1,0:T(8,128)(2,1)S(1)}, bf16[128,1152]{1,0:T(8,128)(2,1)S(1)}, u32[]{:S(2)}, u32[]{:S(2)}) %collective-permute-start.39) | collective-permute-done | bytes 294944 | tf_op jit(solution)/shard_map/ppermute | solution.py:35
  264.1 4.7 collective-permute-done.40
  275.2 6.6 %collective-permute-done.34 = bf16[128,1152]{1,0:T(8,128)(2,1)S(1)} collective-permute-done((bf16[128,1152]{1,0:T(8,128)(2,1)S(1)}, bf16[128,1152]{1,0:T(8,128)(2,1)S(1)}, u32[]{:S(2)}, u32[]{:S(2)}) %collective-permute-start.34) | collective-permute-done | bytes 294944 | tf_op jit(solution)/shard_map/ppermute | solution.py:35
  314.9 4.9 multiply_reduce_fusion
  319.9 5.1 multiply_convert_fusion
  327.3 4.9 fusion.27
  347.6 3.9 collective-permute-done.52
  380.3 3.9 collective-permute-done.57
  476.6 8.2 %collective-permute-done.85 = bf16[144,1152]{1,0:T(8,128)(2,1)S(1)} collective-permute-done((bf16[144,1152]{1,0:T(8,128)(2,1)S(1)}, bf16[144,1152]{1,0:T(8,128)(2,1)S(1)}, u32[]{:S(2)}, u32[]{:S(2)}) %collective-permute-start.85) | collective-permute-done | bytes 331808 | tf_op jit(solution)/shard_map/ppermute | solution.py:35
  517.8 20.9 %collective-permute-start.102 = (bf16[36,1152]{1,0:T(8,128)(2,1)}, bf16[36,1152]{1,0:T(8,128)(2,1)}, u32[]{:S(2)}, u32[]{:S(2)}) collective-permute-start(bf16[36,1152]{1,0:T(8,128)(2,1)} %get-tuple-element.195), channel_id=1, source_target_pairs={{0,4},{2,6},{4,0},{6,2},{1,5},{3,7},{5,1},{7,3},{8,12},{10,14},{12... | collective-permute-start | bytes 248840 | tf_op jit(solution)/shard_map/ppermute | solution.py:35
  551.2 8.0 %collective-permute-start.88 = (bf16[36,1152]{1,0:T(8,128)(2,1)}, bf16[36,1152]{1,0:T(8,128)(2,1)S(1)}, u32[]{:S(2)}, u32[]{:S(2)}) collective-permute-start(bf16[36,1152]{1,0:T(8,128)(2,1)} %get-tuple-element.198), channel_id=1, source_target_pairs={{0,4},{2,6},{4,0},{6,2},{1,5},{3,7},{5,1},{7,3},{8,12},{10,14},{12... | collective-permute-start | bytes 248840 | tf_op jit(solution)/shard_map/ppermute | solution.py:35
  (649 shorter events, 405.4 us)
Async XLA Ops:
  5.0 55.0 %collective-permute-start.7 = (bf16[288,720]{1,0:T(8,128)(2,1)}, bf16[288,720]{1,0:T(8,128)(2,1)}, u32[]{:S(2)}, u32[]{:S(2)}) collective-permute-start(bf16[288,720]{1,0:T(8,128)(2,1)} %pad_maximum_fusion.7), channel_id=1, source_target_pairs={{0,24},{8,16},{16,8},{24,0},{1,25},{9,17},{17,9},{25,1},{2,26},{10... | collective-permute-start | bytes 1244168 | tf_op jit(solution)/shard_map/ppermute | solution.py:35
  8.9 51.2 %collective-permute-start.8 = (bf16[288,720]{1,0:T(8,128)(2,1)}, bf16[288,720]{1,0:T(8,128)(2,1)}, u32[]{:S(2)}, u32[]{:S(2)}) collective-permute-start(bf16[288,720]{1,0:T(8,128)(2,1)} %pad_maximum_fusion.7), channel_id=1, source_target_pairs={{0,16},{8,24},{16,0},{24,8},{1,17},{9,25},{17,1},{25,9},{2,18},{10... | collective-permute-start | bytes 1244168 | tf_op jit(solution)/shard_map/ppermute | solution.py:35
  25.4 34.7 %collective-permute-start.9 = (bf16[288,720]{1,0:T(8,128)(2,1)}, bf16[288,720]{1,0:T(8,128)(2,1)}, u32[]{:S(2)}, u32[]{:S(2)}) collective-permute-start(bf16[288,720]{1,0:T(8,128)(2,1)} %pad_maximum_fusion.7), channel_id=1, source_target_pairs={{0,8},{8,0},{16,24},{24,16},{1,9},{9,1},{17,25},{25,17},{2,10},{10... | collective-permute-start | bytes 1244168 | tf_op jit(solution)/shard_map/ppermute | solution.py:35
  52.5 95.5 %collective-permute-start.14 = (bf16[3,144,1152]{2,1,0:T(8,128)(2,1)}, bf16[3,144,1152]{2,1,0:T(8,128)(2,1)}, u32[]{:S(2)}, u32[]{:S(2)}) collective-permute-start(bf16[3,144,1152]{2,1,0:T(8,128)(2,1)} %fusion.46), channel_id=1, source_target_pairs={{0,8},{8,0},{16,24},{24,16},{1,9},{9,1},{17,25},{25,17},{2,10},{10... | collective-permute-start | bytes 2985992 | tf_op jit(solution)/shard_map/ppermute | solution.py:35
  58.1 94.4 %collective-permute-start.16 = (bf16[3,144,1152]{2,1,0:T(8,128)(2,1)}, bf16[3,144,1152]{2,1,0:T(8,128)(2,1)}, u32[]{:S(2)}, u32[]{:S(2)}) collective-permute-start(bf16[3,144,1152]{2,1,0:T(8,128)(2,1)} %fusion.46), channel_id=1, source_target_pairs={{0,16},{8,24},{16,0},{24,8},{1,17},{9,25},{17,1},{25,9},{2,18},{10... | collective-permute-start | bytes 2985992 | tf_op jit(solution)/shard_map/ppermute | solution.py:35
  83.3 76.4 %collective-permute-start.18 = (bf16[3,144,1152]{2,1,0:T(8,128)(2,1)}, bf16[3,144,1152]{2,1,0:T(8,128)(2,1)}, u32[]{:S(2)}, u32[]{:S(2)}) collective-permute-start(bf16[3,144,1152]{2,1,0:T(8,128)(2,1)} %fusion.46), channel_id=1, source_target_pairs={{0,24},{8,16},{16,8},{24,0},{1,25},{9,17},{17,9},{25,1},{2,26},{10... | collective-permute-start | bytes 2985992 | tf_op jit(solution)/shard_map/ppermute | solution.py:35
  84.6 29.0 %collective-permute-start.29 = (bf16[144,1152]{1,0:T(8,128)(2,1)S(1)}, bf16[144,1152]{1,0:T(8,128)(2,1)S(1)}, u32[]{:S(2)}, u32[]{:S(2)}) collective-permute-start(bf16[144,1152]{1,0:T(8,128)(2,1)S(1)} %copy-done.54), channel_id=1, source_target_pairs={{0,16},{8,24},{16,0},{24,8},{1,17},{9,25},{17,1},{25,9},{2,18},{10... | collective-permute-start | bytes 995336 | tf_op jit(solution)/shard_map/ppermute | solution.py:35
  87.0 28.1 %collective-permute-start.28 = (bf16[144,1152]{1,0:T(8,128)(2,1)S(1)}, bf16[144,1152]{1,0:T(8,128)(2,1)S(1)}, u32[]{:S(2)}, u32[]{:S(2)}) collective-permute-start(bf16[144,1152]{1,0:T(8,128)(2,1)S(1)} %collective-permute-done.27), channel_id=1, source_target_pairs={{0,1},{1,0},{2,3},{3,2},{4,5},{5,4},{6,7},{7,6},{8,9},{9,8},{10,11... | collective-permute-start | bytes 995336 | tf_op jit(solution)/shard_map/ppermute | solution.py:35
  159.7 65.0 %collective-permute-start.36 = (bf16[128,1152]{1,0:T(8,128)(2,1)}, bf16[128,1152]{1,0:T(8,128)(2,1)}, u32[]{:S(2)}, u32[]{:S(2)}) collective-permute-start(bf16[128,1152]{1,0:T(8,128)(2,1)} %fusion.78), channel_id=1, source_target_pairs={{0,8},{8,0},{16,24},{24,16},{1,9},{9,1},{17,25},{25,17},{2,10},{10... | collective-permute-start | bytes 884744 | tf_op jit(solution)/shard_map/ppermute | solution.py:35
  161.2 63.5 %collective-permute-start.37 = (bf16[128,1152]{1,0:T(8,128)(2,1)}, bf16[128,1152]{1,0:T(8,128)(2,1)}, u32[]{:S(2)}, u32[]{:S(2)}) collective-permute-start(bf16[128,1152]{1,0:T(8,128)(2,1)} %fusion.78), channel_id=1, source_target_pairs={{0,16},{8,24},{16,0},{24,8},{1,17},{9,25},{17,1},{25,9},{2,18},{10... | collective-permute-start | bytes 884744 | tf_op jit(solution)/shard_map/ppermute | solution.py:35
  228.4 188.0 %collective-permute-start.111 = (bf16[576,1152]{1,0:T(8,128)(2,1)}, bf16[576,1152]{1,0:T(8,128)(2,1)}, u32[]{:S(2)}, u32[]{:S(2)}) collective-permute-start(bf16[576,1152]{1,0:T(8,128)(2,1)} %convolution_convert_fusion), channel_id=1, source_target_pairs={{0,1},{1,0},{2,3},{3,2},{4,5},{5,4},{6,7},{7,6},{8,9},{9,8},{10,11... | collective-permute-start | bytes 3981320 | tf_op jit(solution)/shard_map/ppermute | solution.py:35
  252.0 169.4 %collective-permute-start.104 = (bf16[576,1152]{1,0:T(8,128)(2,1)}, bf16[576,1152]{1,0:T(8,128)(2,1)}, u32[]{:S(2)}, u32[]{:S(2)}) collective-permute-start(bf16[576,1152]{1,0:T(8,128)(2,1)} %convolution_convert_fusion.1), channel_id=1, source_target_pairs={{0,1},{1,0},{2,3},{3,2},{4,5},{5,4},{6,7},{7,6},{8,9},{9,8},{10,11... | collective-permute-start | bytes 3981320 | tf_op jit(solution)/shard_map/ppermute | solution.py:35
  310.2 30.3 %collective-permute-start.50 = (bf16[4,288,120]{2,1,0:T(8,128)(2,1)}, bf16[4,288,120]{2,1,0:T(8,128)(2,1)}, u32[]{:S(2)}, u32[]{:S(2)}) collective-permute-start(bf16[4,288,120]{2,1,0:T(8,128)(2,1)} %fusion.101), channel_id=1, source_target_pairs={{0,1},{1,0},{2,3},{3,2},{4,5},{5,4},{6,7},{7,6},{8,9},{9,8},{10,11... | collective-permute-start | bytes 829448 | tf_op jit(solution)/shard_map/ppermute | solution.py:35
  416.4 54.1 %collective-permute-start.46 = (bf16[4,128,1152]{2,1,0:T(8,128)(2,1)}, bf16[4,128,1152]{2,1,0:T(8,128)(2,1)}, u32[]{:S(2)}, u32[]{:S(2)}) collective-permute-start(bf16[4,128,1152]{2,1,0:T(8,128)(2,1)} %bitcast.96), channel_id=1, source_target_pairs={{0,1},{1,0},{2,3},{3,2},{4,5},{5,4},{6,7},{7,6},{8,9},{9,8},{10,11... | collective-permute-start | bytes 3538952 | tf_op jit(solution)/shard_map/ppermute | solution.py:35
  421.4 40.0 %collective-permute-start.112 = (bf16[144,1152]{1,0:T(8,128)(2,1)}, bf16[144,1152]{1,0:T(8,128)(2,1)}, u32[]{:S(2)}, u32[]{:S(2)}) collective-permute-start(bf16[144,1152]{1,0:T(8,128)(2,1)} %get-tuple-element.141), channel_id=1, source_target_pairs={{0,2},{2,0},{4,6},{6,4},{1,3},{3,1},{5,7},{7,5},{8,10},{10,8},{12,... | collective-permute-start | bytes 995336 | tf_op jit(solution)/shard_map/ppermute | solution.py:35
  440.2 25.0 %collective-permute-start.113 = (bf16[144,1152]{1,0:T(8,128)(2,1)}, bf16[144,1152]{1,0:T(8,128)(2,1)}, u32[]{:S(2)}, u32[]{:S(2)}) collective-permute-start(bf16[144,1152]{1,0:T(8,128)(2,1)} %get-tuple-element.143), channel_id=1, source_target_pairs={{0,4},{2,6},{4,0},{6,2},{1,5},{3,7},{5,1},{7,3},{8,12},{10,14},{12... | collective-permute-start | bytes 995336 | tf_op jit(solution)/shard_map/ppermute | solution.py:35
  450.7 23.8 %collective-permute-start.84 = (bf16[144,1152]{1,0:T(8,128)(2,1)}, bf16[144,1152]{1,0:T(8,128)(2,1)}, u32[]{:S(2)}, u32[]{:S(2)}) collective-permute-start(bf16[144,1152]{1,0:T(8,128)(2,1)} %get-tuple-element.155), channel_id=1, source_target_pairs={{0,8},{8,0},{16,24},{24,16},{1,9},{9,1},{17,25},{25,17},{2,10},{10... | collective-permute-start | bytes 995336 | tf_op jit(solution)/shard_map/ppermute | solution.py:35
  461.4 23.5 %collective-permute-start.85 = (bf16[144,1152]{1,0:T(8,128)(2,1)S(1)}, bf16[144,1152]{1,0:T(8,128)(2,1)S(1)}, u32[]{:S(2)}, u32[]{:S(2)}) collective-permute-start(bf16[144,1152]{1,0:T(8,128)(2,1)S(1)} %copy-done.59), channel_id=1, source_target_pairs={{0,16},{8,24},{16,0},{24,8},{1,17},{9,25},{17,1},{25,9},{2,18},{10... | collective-permute-start | bytes 995336 | tf_op jit(solution)/shard_map/ppermute | solution.py:35
  492.0 25.8 %collective-permute-start.109 = (bf16[144,1152]{1,0:T(8,128)(2,1)}, bf16[144,1152]{1,0:T(8,128)(2,1)}, u32[]{:S(2)}, u32[]{:S(2)}) collective-permute-start(bf16[144,1152]{1,0:T(8,128)(2,1)} %bitcast.585), channel_id=1, source_target_pairs={{0,4},{2,6},{4,0},{6,2},{1,5},{3,7},{5,1},{7,3},{8,12},{10,14},{12... | collective-permute-start | bytes 995336 | tf_op jit(solution)/shard_map/ppermute | solution.py:35
  505.3 35.4 %collective-permute-start.47 = (bf16[128,1152]{1,0:T(8,128)(2,1)}, bf16[128,1152]{1,0:T(8,128)(2,1)}, u32[]{:S(2)}, u32[]{:S(2)}) collective-permute-start(bf16[128,1152]{1,0:T(8,128)(2,1)} %get-tuple-element.166), channel_id=1, source_target_pairs={{0,2},{2,0},{4,6},{6,4},{1,3},{3,1},{5,7},{7,5},{8,10},{10,8},{12,... | collective-permute-start | bytes 884744 | tf_op jit(solution)/shard_map/ppermute | solution.py:35
  505.4 41.0 %collective-permute-start.48 = (bf16[128,1152]{1,0:T(8,128)(2,1)}, bf16[128,1152]{1,0:T(8,128)(2,1)}, u32[]{:S(2)}, u32[]{:S(2)}) collective-permute-start(bf16[128,1152]{1,0:T(8,128)(2,1)} %get-tuple-element.168), channel_id=1, source_target_pairs={{0,4},{2,6},{4,0},{6,2},{1,5},{3,7},{5,1},{7,3},{8,12},{10,14},{12... | collective-permute-start | bytes 884744 | tf_op jit(solution)/shard_map/ppermute | solution.py:35
  512.4 33.9 %collective-permute-start.49 = (bf16[128,1152]{1,0:T(8,128)(2,1)S(1)}, bf16[128,1152]{1,0:T(8,128)(2,1)S(1)}, u32[]{:S(2)}, u32[]{:S(2)}) collective-permute-start(bf16[128,1152]{1,0:T(8,128)(2,1)S(1)} %copy-done.61), channel_id=1, source_target_pairs={{0,6},{2,4},{4,2},{6,0},{1,7},{3,5},{5,3},{7,1},{8,14},{10,12},{12... | collective-permute-start | bytes 884744 | tf_op jit(solution)/shard_map/ppermute | solution.py:35
  517.8 41.4 %collective-permute-start.101 = (bf16[36,1152]{1,0:T(8,128)(2,1)}, bf16[36,1152]{1,0:T(8,128)(2,1)}, u32[]{:S(2)}, u32[]{:S(2)}) collective-permute-start(bf16[36,1152]{1,0:T(8,128)(2,1)} %get-tuple-element.193), channel_id=1, source_target_pairs={{0,2},{2,0},{4,6},{6,4},{1,3},{3,1},{5,7},{7,5},{8,10},{10,8},{12,... | collective-permute-start | bytes 248840 | tf_op jit(solution)/shard_map/ppermute | solution.py:35
  517.8 43.6 %collective-permute-start.102 = (bf16[36,1152]{1,0:T(8,128)(2,1)}, bf16[36,1152]{1,0:T(8,128)(2,1)}, u32[]{:S(2)}, u32[]{:S(2)}) collective-permute-start(bf16[36,1152]{1,0:T(8,128)(2,1)} %get-tuple-element.195), channel_id=1, source_target_pairs={{0,4},{2,6},{4,0},{6,2},{1,5},{3,7},{5,1},{7,3},{8,12},{10,14},{12... | collective-permute-start | bytes 248840 | tf_op jit(solution)/shard_map/ppermute | solution.py:35
  (189 other events, 2345.3 us)
